TPU v7x, 512 devices: a whole 4x4x16 slice. The times are simulated.
512 devices in a mesh: seq: 16 (over z_lo, y), col: 32 (over z_hi, x, core).
Axes of the slice: x: 4, y: 4, z: 16 (z_hi: 4, z_lo: 4; z = z_hi * 4 + z_lo), core: 2. Of those that a mesh axis runs over, the one named last changes fastest.
Arguments:
- layer_in: bfloat16 [512, 256, 768], P('seq', 'col'), may hold values from -13.5 to 13.5
- cotangent: bfloat16 [512, 256, 768], P('seq', 'col'), may hold values from -6 to 6
- w_query: bfloat16 [768, 384], replicated, may hold values from -0.21875 to 0.21875
- w_key: bfloat16 [768, 384], replicated, may hold values from -0.21875 to 0.21875
- w_value: bfloat16 [768, 384], replicated, may hold values from -0.21875 to 0.21875
- w_out: bfloat16 [384, 768], replicated, may hold values from -0.3125 to 0.3125
Outputs:
- layer_out: bfloat16 [512, 256, 768], P('seq', 'col')
- input_grad: bfloat16 [512, 256, 768], P('seq', 'col')
All inputs are finite; a program needn't handle non-finite values.
Results may differ from a plain program's by a relative error of at most 0.025.
Values may be sent and summed in bfloat16 or wider, within the bound.
No kernel may reach another device: no remote copies, remote signals or barrier semaphores. Data moves between devices by JAX's collectives and lax.ppermute only.
A program may use at most 64 MiB of HBM per device.

v0:
```python
import math

import jax
import jax.numpy as jnp
from jax import lax
from jax.sharding import PartitionSpec as P

H = 6
DH = 64


def project(tokens, weight):
    in_shape = tokens.shape
    result = jnp.dot(tokens.reshape(-1, in_shape[-1]), weight, preferred_element_type=jnp.float32)
    return result.astype(jnp.bfloat16).reshape(in_shape[:-1] + (weight.shape[1],))


def back_project(tokens, weight):
    in_shape = tokens.shape
    result = lax.dot_general(
        tokens.reshape(-1, in_shape[-1]),
        weight,
        (((1,), (1,)), ((), ())),
        preferred_element_type=jnp.float32,
    )
    return result.astype(jnp.bfloat16).reshape(in_shape[:-1] + (weight.shape[0],))


def split_heads(tokens):
    return tokens.reshape(tokens.shape[0], tokens.shape[1], H, tokens.shape[2] // H)


def tied_forward(queries, keys_rows, scaling):
    q_heads = split_heads(queries)
    k_heads = split_heads(keys_rows)
    partial_value = jnp.einsum(
        "rihe,rjhe->hij", q_heads, k_heads, preferred_element_type=jnp.float32
    )
    d_prob = None
    logits = lax.psum(partial_value, ("seq", "col")) * scaling
    attn_probs = jax.nn.softmax(logits, axis=-1).astype(jnp.bfloat16)
    return (attn_probs, attn_probs, d_prob)


def mix_values(attn_probs, values):
    attended = jnp.einsum(
        "hij,rjhe->rihe", attn_probs, split_heads(values), preferred_element_type=jnp.float32
    )
    return attended.astype(jnp.bfloat16).reshape(values.shape)


def tied_backward(values, d_att, attn_probs, scaling):
    partial_value = jnp.einsum(
        "rihe,rjhe->hij",
        split_heads(d_att),
        split_heads(values),
        preferred_element_type=jnp.float32,
    )
    d_total = lax.psum(partial_value, ("seq", "col"))
    prob_f32 = attn_probs.astype(jnp.float32)
    d_logit = prob_f32 * (d_total - jnp.sum(prob_f32 * d_total, axis=-1, keepdims=True)) * scaling
    d_logit = d_logit.astype(jnp.bfloat16)
    return d_logit


def input_side(queries, keys_rows, d_att, attn_probs, d_logit):
    q_heads = split_heads(queries)
    k_heads = split_heads(keys_rows)
    a_heads = split_heads(d_att)
    d_query = jnp.einsum("hij,rjhe->rihe", d_logit, k_heads, preferred_element_type=jnp.float32)
    d_key = jnp.einsum("hij,rihe->rjhe", d_logit, q_heads, preferred_element_type=jnp.float32)
    d_value = jnp.einsum("hij,rihe->rjhe", attn_probs, a_heads, preferred_element_type=jnp.float32)
    return jnp.concatenate(
        (
            d_query.astype(jnp.bfloat16).reshape(queries.shape),
            d_key.astype(jnp.bfloat16).reshape(queries.shape),
            d_value.astype(jnp.bfloat16).reshape(queries.shape),
        ),
        axis=2,
    )


def shards(layer_in, cotangent, w_query, w_key, w_value, w_out):
    rows_total = layer_in.shape[0] * lax.axis_size("seq")
    scaling = 1.0 / math.sqrt(DH * rows_total)
    stacked = jnp.concatenate((w_query, w_key, w_value), axis=1)
    queries = project(layer_in, w_query)
    keys_rows = project(layer_in, w_key)
    values = project(layer_in, w_value)
    queries, keys_rows, values = (
        lax.all_to_all(queries, "col", split_axis=0, concat_axis=1, tiled=True),
        lax.all_to_all(keys_rows, "col", split_axis=0, concat_axis=1, tiled=True),
        lax.all_to_all(values, "col", split_axis=0, concat_axis=1, tiled=True),
    )
    d_att = lax.all_to_all(
        back_project(cotangent, w_out), "col", split_axis=0, concat_axis=1, tiled=True
    )
    attn_probs, prob_share, d_prob = tied_forward(queries, keys_rows, scaling)
    attended = mix_values(attn_probs, values)
    d_logit = tied_backward(values, d_att, attn_probs, scaling)
    gradients = input_side(queries, keys_rows, d_att, attn_probs, d_logit)
    attended = lax.all_to_all(attended, "col", split_axis=1, concat_axis=0, tiled=True)
    layer_out = project(attended, w_out)
    gradients = lax.all_to_all(gradients, "col", split_axis=1, concat_axis=0, tiled=True)
    input_grad = back_project(gradients, stacked)
    return (layer_out, input_grad)


def solution(mesh):
    placed = (P("seq", "col", None), P("seq", "col", None), P(), P(), P(), P())
    return jax.shard_map(
        shards,
        mesh=mesh,
        in_specs=placed,
        out_specs=(P("seq", "col", None), P("seq", "col", None)),
        check_vma=False,
    )
```

profile of v0, /device:TPU:1, one launch (start us, length us, event | category | flops | bytes accessed | tf_op | source)
XLA Modules:
  0.0 695.3 jit_solution(9967883519032573637)
XLA Ops:
  7.2 2.4 fusion.21
  9.6 19.2 %all-to-all-start.1 = ((bf16[32,8,384]{2,1,0:T(8,128)(2,1)}), bf16[32,8,384]{2,1,0:T(8,128)(2,1)S(1)}, u32[]{:S(2)}, u32[]{:S(2)}) async-start(bf16[32,8,384]{2,1,0:T(8,128)(2,1)} %fusion.21), calls=%async_computation.1 | async-start | bytes 393216 | tf_op jit(solution)/shard_map/all_to_all | solution.py:91
  29.9 18.4 %all-to-all-done.1 = bf16[32,8,384]{2,1,0:T(8,128)(2,1)S(1)} async-done(((bf16[32,8,384]{2,1,0:T(8,128)(2,1)}), bf16[32,8,384]{2,1,0:T(8,128)(2,1)S(1)}, u32[]{:S(2)}, u32[]{:S(2)}) %all-to-all-start.1) | async-done | bytes 196640 | tf_op jit(solution)/shard_map/all_to_all | solution.py:91
  48.3 5.2 all-to-all-start.2
  54.6 16.0 %all-to-all-done.2 = bf16[32,8,384]{2,1,0:T(8,128)(2,1)S(1)} async-done(((bf16[32,8,384]{2,1,0:T(8,128)(2,1)}), bf16[32,8,384]{2,1,0:T(8,128)(2,1)S(1)}, u32[]{:S(2)}, u32[]{:S(2)}) %all-to-all-start.2) | async-done | bytes 196640 | tf_op jit(solution)/shard_map/all_to_all | solution.py:92
  70.6 7.5 %all-to-all-start = ((bf16[32,8,384]{2,1,0:T(8,128)(2,1)}), bf16[32,8,384]{2,1,0:T(8,128)(2,1)S(1)}, u32[]{:S(2)}, u32[]{:S(2)}) async-start(bf16[32,8,384]{2,1,0:T(8,128)(2,1)} %fusion.20), calls=%async_computation | async-start | bytes 393216 | tf_op jit(solution)/shard_map/all_to_all | solution.py:93
  79.2 15.6 %all-to-all-done = bf16[32,8,384]{2,1,0:T(8,128)(2,1)S(1)} async-done(((bf16[32,8,384]{2,1,0:T(8,128)(2,1)}), bf16[32,8,384]{2,1,0:T(8,128)(2,1)S(1)}, u32[]{:S(2)}, u32[]{:S(2)}) %all-to-all-start) | async-done | bytes 196640 | tf_op jit(solution)/shard_map/all_to_all | solution.py:93
  94.8 7.0 %all-to-all-start.4 = ((bf16[32,8,384]{2,1,0:T(8,128)(2,1)}), bf16[32,8,384]{2,1,0:T(8,128)(2,1)S(1)}, u32[]{:S(2)}, u32[]{:S(2)}) async-start(bf16[32,8,384]{2,1,0:T(8,128)(2,1)} %fusion.23), calls=%async_computation.4 | async-start | bytes 393216 | tf_op jit(solution)/shard_map/all_to_all | solution.py:95
  103.6 15.0 %all-to-all-done.4 = bf16[32,8,384]{2,1,0:T(8,128)(2,1)S(1)} async-done(((bf16[32,8,384]{2,1,0:T(8,128)(2,1)}), bf16[32,8,384]{2,1,0:T(8,128)(2,1)S(1)}, u32[]{:S(2)}, u32[]{:S(2)}) %all-to-all-start.4) | async-done | bytes 196640 | tf_op jit(solution)/shard_map/all_to_all | solution.py:95
  119.3 1.6 fusion.44
  120.8 1.6 fusion.45
  122.4 478.3 %all-reduce.3.cloned.1.call-done = (f32[6,256,256]{2,1,0:T(8,128)}, f32[6,256,256]{2,1,0:T(8,128)}) async-done(((f32[6,256,256]{2,1,0:T(8,128)}, f32[6,256,256]{2,1,0:T(8,128)}), (f32[6,256,256]{2,1,0:T(8,128)}, f32[6,256,256]{2,1,0:T(8,128)})) %all-reduce.3.cloned.1.call-update) | async-done | bytes 3145744 | tf_op jit(solution)/shard_map/psum | solution.py:40
  600.8 2.1 fusion.42
  603.1 2.4 convolution_convert_fusion.3
  605.6 2.4 convolution_convert_fusion.2
  610.2 1.8 reduce
  612.8 14.1 %all-to-all-start.3 = ((bf16[32,2,1536]{2,1,0:T(2,128)(2,1)}), bf16[32,2,1536]{2,1,0:T(2,128)(2,1)S(1)}, u32[]{:S(2)}, u32[]{:S(2)}) async-start(bf16[32,2,1536]{2,1,0:T(2,128)(2,1)} %reshape.133), calls=%async_computation.3 | async-start | bytes 393216 | tf_op jit(solution)/shard_map/all_to_all | solution.py:102
  627.7 1.3 fusion.43
  629.0 4.2 reduce.1
  634.3 10.8 %all-to-all-done.3 = bf16[32,2,1536]{2,1,0:T(2,128)(2,1)S(1)} async-done(((bf16[32,2,1536]{2,1,0:T(2,128)(2,1)}), bf16[32,2,1536]{2,1,0:T(2,128)(2,1)S(1)}, u32[]{:S(2)}, u32[]{:S(2)}) %all-to-all-start.3) | async-done | bytes 196640 | tf_op jit(solution)/shard_map/all_to_all | solution.py:102
  645.1 5.5 all-to-all-start.5
  650.8 1.1 fusion.19
  651.9 33.5 %all-to-all-done.5 = bf16[32,2,4608]{2,1,0:T(2,128)(2,1)S(1)} async-done(((bf16[32,2,4608]{2,1,0:T(2,128)(2,1)}), bf16[32,2,4608]{2,1,0:T(2,128)(2,1)S(1)}, u32[]{:S(2)}, u32[]{:S(2)}) %all-to-all-start.5) | async-done | bytes 589856 | tf_op jit(solution)/shard_map/all_to_all | solution.py:104
  685.9 2.5 fusion.16
  (39 shorter events, 11.2 us)
Async XLA Ops:
  7.2 70.9 %copy-start = (bf16[384,768]{1,0:T(8,128)(2,1)S(1)}, bf16[384,768]{1,0:T(8,128)(2,1)}, u32[]{:S(2)}) copy-start(bf16[384,768]{1,0:T(8,128)(2,1)} %param.11) | copy-start | bytes 1769476
  7.2 21.6 %copy-start.1 = (bf16[32,8,768]{2,1,0:T(8,128)(2,1)S(1)}, bf16[32,8,768]{2,1,0:T(8,128)(2,1)}, u32[]{:S(2)}) copy-start(bf16[32,8,768]{2,1,0:T(8,128)(2,1)} %param.6) | copy-start | bytes 1179652
  7.2 21.6 %copy-start.5 = (bf16[768,384]{1,0:T(8,128)(2,1)S(1)}, bf16[768,384]{1,0:T(8,128)(2,1)}, u32[]{:S(2)}) copy-start(bf16[768,384]{1,0:T(8,128)(2,1)} %param.9) | copy-start | bytes 1769476
  7.2 46.3 %copy-start.2 = (bf16[768,384]{1,0:T(8,128)(2,1)S(1)}, bf16[768,384]{1,0:T(8,128)(2,1)}, u32[]{:S(2)}) copy-start(bf16[768,384]{1,0:T(8,128)(2,1)} %param.10) | copy-start | bytes 1769476
  9.6 38.7 %all-to-all-start.1 = ((bf16[32,8,384]{2,1,0:T(8,128)(2,1)}), bf16[32,8,384]{2,1,0:T(8,128)(2,1)S(1)}, u32[]{:S(2)}, u32[]{:S(2)}) async-start(bf16[32,8,384]{2,1,0:T(8,128)(2,1)} %fusion.21), calls=%async_computation.1 | async-start | bytes 393216 | tf_op jit(solution)/shard_map/all_to_all | solution.py:91
  28.8 49.3 %copy-start.6 = (bf16[32,8,768]{2,1,0:T(8,128)(2,1)S(1)}, bf16[32,8,768]{2,1,0:T(8,128)(2,1)}, u32[]{:S(2)}) copy-start(bf16[32,8,768]{2,1,0:T(8,128)(2,1)} %param.7) | copy-start | bytes 1179652
  48.3 22.3 %all-to-all-start.2 = ((bf16[32,8,384]{2,1,0:T(8,128)(2,1)}), bf16[32,8,384]{2,1,0:T(8,128)(2,1)S(1)}, u32[]{:S(2)}, u32[]{:S(2)}) async-start(bf16[32,8,384]{2,1,0:T(8,128)(2,1)} %fusion.22), calls=%async_computation.2 | async-start | bytes 393216 | tf_op jit(solution)/shard_map/all_to_all | solution.py:92
  70.6 24.2 %all-to-all-start = ((bf16[32,8,384]{2,1,0:T(8,128)(2,1)}), bf16[32,8,384]{2,1,0:T(8,128)(2,1)S(1)}, u32[]{:S(2)}, u32[]{:S(2)}) async-start(bf16[32,8,384]{2,1,0:T(8,128)(2,1)} %fusion.20), calls=%async_computation | async-start | bytes 393216 | tf_op jit(solution)/shard_map/all_to_all | solution.py:93
  94.8 23.9 %all-to-all-start.4 = ((bf16[32,8,384]{2,1,0:T(8,128)(2,1)}), bf16[32,8,384]{2,1,0:T(8,128)(2,1)S(1)}, u32[]{:S(2)}, u32[]{:S(2)}) async-start(bf16[32,8,384]{2,1,0:T(8,128)(2,1)} %fusion.23), calls=%async_computation.4 | async-start | bytes 393216 | tf_op jit(solution)/shard_map/all_to_all | solution.py:95
  101.8 498.9 %all-reduce.3.cloned.1.call-start = ((), (), s32[]{:S(2)}) async-start(), calls=%async_computation.6 | async-start | bytes 6291456 | tf_op jit(solution)/shard_map/psum | solution.py:40
  612.8 32.3 %all-to-all-start.3 = ((bf16[32,2,1536]{2,1,0:T(2,128)(2,1)}), bf16[32,2,1536]{2,1,0:T(2,128)(2,1)S(1)}, u32[]{:S(2)}, u32[]{:S(2)}) async-start(bf16[32,2,1536]{2,1,0:T(2,128)(2,1)} %reshape.133), calls=%async_computation.3 | async-start | bytes 393216 | tf_op jit(solution)/shard_map/all_to_all | solution.py:102
  645.1 40.3 %all-to-all-start.5 = ((bf16[32,2,4608]{2,1,0:T(2,128)(2,1)}), bf16[32,2,4608]{2,1,0:T(2,128)(2,1)S(1)}, u32[]{:S(2)}, u32[]{:S(2)}) async-start(bf16[32,2,4608]{2,1,0:T(2,128)(2,1)} %reshape.135), calls=%async_computation.5 | async-start | bytes 1179648 | tf_op jit(solution)/shard_map/all_to_all | solution.py:104
  650.8 35.2 %copy-start.3 = (bf16[768,384]{1,0:T(8,128)(2,1)S(1)}, bf16[768,384]{1,0:T(8,128)(2,1)}, u32[]{:S(2)}) copy-start(bf16[768,384]{1,0:T(8,128)(2,1)} %param.10) | copy-start | bytes 1769476
  650.8 35.2 %copy-start.4 = (bf16[768,384]{1,0:T(8,128)(2,1)S(1)}, bf16[768,384]{1,0:T(8,128)(2,1)}, u32[]{:S(2)}) copy-start(bf16[768,384]{1,0:T(8,128)(2,1)} %param.8) | copy-start | bytes 1769476
Sparse Core Ops, SparseCore 0:
  122.5 478.1 all-reduce.2
where the time goes:
time: 696 us; the launch traced here: 695 us
  waiting for transfers between devices  588 us (84%)
  starting transfers between devices  58.6 us (8%)
  matrix products  17.8 us (3%)
  between operations  14.3 us (2%)
  other arithmetic  9.68 us (1%)
  local copies, waits for them, and re-layouts  7.11 us (1%)
    psum x1, waiting for transfers between devices, tied_forward(): logits = lax.psum(partial_value, ('seq', 'col')) * scaling  478 us
    all_to_all x1, waiting for transfers between devices, shards(): lax.all_to_all(gradients, 'col', split_axis=1, concat_axis=0, tiled=True)  33.5 us
    all_to_all x1, starting transfers between devices, shards(): lax.all_to_all(queries, 'col', split_axis=0, concat_axis=1, tiled=True)  19.2 us
    all_to_all x1, waiting for transfers between devices, shards(): lax.all_to_all(queries, 'col', split_axis=0, concat_axis=1, tiled=True)  18.4 us
    all_to_all x1, waiting for transfers between devices, shards(): lax.all_to_all(keys_rows, 'col', split_axis=0, concat_axis=1, tiled=True)  16 us
    all_to_all x1, waiting for transfers between devices, shards(): lax.all_to_all(values, 'col', split_axis=0, concat_axis=1, tiled=True)  15.6 us
    all_to_all x1, waiting for transfers between devices, shards(): lax.all_to_all(back_project(cotangent, w_out), 'col', split_axis=0, conca...  15 us
    all_to_all x1, starting transfers between devices, shards(): lax.all_to_all(attended, 'col', split_axis=1, concat_axis=0, tiled=True)  14.1 us
  transfers between devices with their start and end apart: 7, of which 7 were waited for; matrix products, arithmetic and copies ran while one was open for 2% of the time, Pallas kernels for 0%

commit v1 on v0

v1 whole, which is shorter than its diff:
```python
import math

import jax
import jax.numpy as jnp
import numpy as np
from jax import lax
from jax.experimental import pallas as pl
from jax.experimental.pallas import tpu as pltpu
from jax.sharding import Mesh, PartitionSpec as P

H = 6
DH = 64
HD = H * DH
D = 768
NT = 32
RE = 512
SCALING = 1.0 / math.sqrt(DH * 512)
X = ("x1", "x0")
I_PAIRS = [(0, 1), (1, 0), (2, 3), (3, 2)]
J_PAIRS = [(0, 3), (3, 0), (1, 2), (2, 1)]
BF = jnp.bfloat16
F32 = jnp.float32


def dot(a, b):
    return jnp.dot(a, b, preferred_element_type=F32)


def dot_t(a, b):
    return lax.dot_general(a, b, (((1,), (1,)), ((), ())), preferred_element_type=F32)


def low_half(shape):
    return lax.broadcasted_iota(jnp.int32, shape, len(shape) - 1) < DH


def roll_half(tile):
    flat = tile.reshape(-1, 2 * DH)
    return pltpu.roll(flat, DH, 1).reshape(tile.shape)


def tokens_to_heads(tokens, put):
    split = tokens.reshape(4, 4, 2, 8, HD)
    keep = low_half((4, 4, 8, 128))
    for tile in range(3):
        first = split[:, :, 0, :, tile * 128 : tile * 128 + 128]
        second = split[:, :, 1, :, tile * 128 : tile * 128 + 128]
        even = jnp.where(keep, first, roll_half(second))
        odd = jnp.where(keep, roll_half(first), second)
        for pair in range(4):
            put(2 * tile, pair, even[:, pair].reshape(NT, 128))
            put(2 * tile + 1, pair, odd[:, pair].reshape(NT, 128))


def heads_to_tokens(heads, scratch):
    keep = low_half((NT, 128))
    for tile in range(3):
        even, odd = heads(2 * tile), heads(2 * tile + 1)
        for pair in range(4):
            a = even[:, pair * 128 : pair * 128 + 128]
            b = odd[:, pair * 128 : pair * 128 + 128]
            first = jnp.where(keep, a, roll_half(b))
            second = jnp.where(keep, roll_half(a), b)
            lanes = slice(tile * 128, tile * 128 + 128)
            scratch[:, 2 * pair, :, lanes] = first.reshape(4, 8, 128)
            scratch[:, 2 * pair + 1, :, lanes] = second.reshape(4, 8, 128)


def call(body, out_shape, scratch=(), flops=0, data=0, scalars=0, inputs=1):
    return pl.pallas_call(
        body,
        out_shape=out_shape,
        in_specs=[pl.BlockSpec(memory_space=pltpu.SMEM)] * scalars
        + [pl.BlockSpec(memory_space=pltpu.VMEM)] * inputs,
        out_specs=jax.tree.map(lambda _: pl.BlockSpec(memory_space=pltpu.VMEM), out_shape),
        scratch_shapes=list(scratch),
        compiler_params=pltpu.CompilerParams(vmem_limit_bytes=40 * 2**20),
        cost_estimate=pl.CostEstimate(flops=flops, bytes_accessed=data, transcendentals=0),
    )


def shaped(shape, dtype):
    return jax.ShapeDtypeStruct(shape, dtype)


def project_body(x_ref, wq_ref, wk_ref, wv_ref, q_ref, kv_ref):
    x = x_ref[...]

    def put_q(h, pair, block):
        q_ref[h, :, pair * 128 : pair * 128 + 128] = block.astype(BF)

    def put_kv(which):
        def put(h, pair, block):
            kv_ref[which, h, :, pair * 128 : pair * 128 + 128] = block.astype(BF)

        return put

    tokens_to_heads(dot(x, wq_ref[...]), put_q)
    tokens_to_heads(dot(x, wk_ref[...]), put_kv(0))
    tokens_to_heads(dot(x, wv_ref[...]), put_kv(1))


def relayout_body(a_ref, out_ref):
    def put(h, pair, block):
        out_ref[h, :, pair * 128 : pair * 128 + 128] = block.astype(BF)

    tokens_to_heads(a_ref[...].astype(F32), put)


def partial_body(par_ref, q, qo, da, dao, kv, kvo, kvc, out_ref, scr):
    par = par_ref[0]
    for h in range(H):
        for which, own, other in ((0, q, qo), (1, da, dao)):
            left = jnp.concatenate([own[h], other[h]], axis=0)
            right = jnp.concatenate([kv[which, h], kvo[which, h], kvc[0, which, h], kvc[1, which, h]], axis=0)
            part = dot_t(left, right)
            rows = slice((which * 3 + h % 3) * 8, (which * 3 + h % 3) * 8 + 8)
            for side in range(2):
                place = lax.bitwise_xor(par, side) * 8 + h // 3
                for zs in range(4):
                    start = side * NT + zs * 8
                    scr[place + 2 * zs, rows, :] = part[start : start + 8]
    out_ref[...] = scr[...].astype(BF)


def sum_body(a_ref, out_ref):
    total = a_ref[0].astype(F32)
    for k in range(1, 16):
        total = total + a_ref[k].astype(F32)
    for k in range(8):
        out_ref[k] = total


def softmax_body(par_ref, g_ref, out_ref):
    total = g_ref[0:2] + g_ref[2:4] + g_ref[4:6] + g_ref[6:8]
    own_first = par_ref[0] == 0
    l0, l1 = total[0, 0:24] * SCALING, total[1, 0:24] * SCALING
    d0, d1 = total[0, 24:48], total[1, 24:48]
    top = jnp.maximum(jnp.max(l0, axis=-1, keepdims=True), jnp.max(l1, axis=-1, keepdims=True))
    e0, e1 = jnp.exp(l0 - top), jnp.exp(l1 - top)
    norm = jnp.sum(e0, axis=-1, keepdims=True) + jnp.sum(e1, axis=-1, keepdims=True)
    p0 = (e0 / norm).astype(BF).astype(F32)
    p1 = (e1 / norm).astype(BF).astype(F32)
    mean = jnp.sum(p0 * d0, axis=-1, keepdims=True) + jnp.sum(p1 * d1, axis=-1, keepdims=True)
    prob = jnp.where(own_first, p0, p1)
    d_prob = jnp.where(own_first, d0, d1)
    d_logit = prob * (d_prob - mean) * SCALING
    both = jnp.concatenate([prob, d_logit], axis=0).astype(BF)
    for k in range(16):
        out_ref[k] = both


def mix_body(par_ref, pd_ref, q, qo, da, dao, kv, kvo, kvc, i_own, i_send, j_own, j_x, j_core, scr):
    par = par_ref[0]
    scr[...] = pd_ref[...].astype(F32)
    for h in range(H):
        probs, d_logits = [], []
        for side in range(2):
            place = lax.bitwise_xor(par, side) * 8 + h // 3
            for zs in range(4):
                probs.append(scr[place + 2 * zs, (h % 3) * 8 : (h % 3) * 8 + 8, :])
                d_logits.append(scr[place + 2 * zs, 24 + (h % 3) * 8 : 24 + (h % 3) * 8 + 8, :])
        prob = jnp.concatenate(probs, axis=0)
        d_logit = jnp.concatenate(d_logits, axis=0)
        keys = jnp.concatenate([kv[0, h], kvo[0, h], kvc[0, 0, h], kvc[1, 0, h]], axis=0)
        values = jnp.concatenate([kv[1, h], kvo[1, h], kvc[0, 1, h], kvc[1, 1, h]], axis=0)
        queries = jnp.concatenate([q[h], qo[h]], axis=0)
        d_att = jnp.concatenate([da[h], dao[h]], axis=0)
        attended = dot(prob.astype(BF), values)
        d_query = dot(d_logit.astype(BF), keys)
        d_key = dot(d_logit.T.astype(BF), queries)
        d_value = dot(prob.T.astype(BF), d_att)
        for which, value in ((0, attended), (1, d_query)):
            i_own[which, h] = value[0:NT]
            i_send[which, h] = value[NT:].astype(BF)
        for which, value in ((0, d_key), (1, d_value)):
            j_own[which, h] = value[0:NT]
            j_x[which, h] = value[NT : 2 * NT]
            j_core[0, which, h] = value[2 * NT : 3 * NT].astype(BF)
            j_core[1, which, h] = value[3 * NT :].astype(BF)


def add_body(j_x, j_core, out_ref):
    out_ref[...] = (j_x[...] + j_core[1].astype(F32)).astype(BF)


def finish_body(i_own, i_recv, j_own, j_core, j_recv, wq_ref, wk_ref, wv_ref, att_ref, grad_ref, scr):
    def gather(heads):
        heads_to_tokens(heads, scr)
        return scr[...].reshape(4 * 8 * 8, HD).astype(BF)

    att_ref[...] = gather(lambda h: i_own[0, h] + i_recv[0, h].astype(F32))
    d_query = gather(lambda h: i_own[1, h] + i_recv[1, h].astype(F32))
    total = dot_t(d_query, wq_ref[...])
    for which, weight in ((0, wk_ref), (1, wv_ref)):
        grad = gather(
            lambda h: j_own[which, h] + j_core[0, which, h].astype(F32) + j_recv[which, h].astype(F32)
        )
        total = total + dot_t(grad, weight[...])
    grad_ref[...] = total.astype(BF)


def shards(layer_in, cotangent, w_query, w_key, w_value, w_out):
    par = lax.axis_index("x0").astype(jnp.int32).reshape(1)
    units = (H, NT, RE)

    def over_z_hi(a):
        return lax.all_to_all(a, "zh", split_axis=0, concat_axis=0, tiled=True)

    with jax.named_scope("layer_in_to_home"):
        x_home = over_z_hi(layer_in).reshape(256, D)
    with jax.named_scope("d_att"):
        d_att = dot_t(cotangent.reshape(256, D), w_out).astype(BF).reshape(32, 8, HD)
        d_att = over_z_hi(d_att).reshape(256, HD)
    with jax.named_scope("project"):
        q, kv = call(
            project_body, (shaped(units, BF), shaped((2,) + units, BF)), flops=2 * 256 * D * 3 * HD, data=3 * 2**20, inputs=4
        )(x_home, w_query, w_key, w_value)
        da = call(relayout_body, shaped(units, BF), data=2**19)(d_att)
    with jax.named_scope("exchange_blocks"):
        qo = lax.ppermute(q, X, I_PAIRS)
        kvo = lax.ppermute(kv, X, J_PAIRS)
        dao = lax.ppermute(da, X, I_PAIRS)
        kvc = lax.ppermute(jnp.stack([kv, kvo]), "core", [(0, 1), (1, 0)])
    with jax.named_scope("partial_sums"):
        part = call(
            partial_body, shaped((16, 48, 128), BF), [pltpu.VMEM((16, 48, 128), F32)],
            flops=2 * 2 * H * 64 * 128 * RE, data=2**21, scalars=1, inputs=7,
        )(par, q, qo, da, dao, kv, kvo, kvc)
    with jax.named_scope("reduce"):
        part = lax.all_to_all(part, ("zh", "zl"), split_axis=0, concat_axis=0, tiled=True)
        part = call(sum_body, shaped((8, 48, 128), F32), data=2**19)(part)
        part = lax.all_to_all(part, ("y", "x0"), split_axis=0, concat_axis=0, tiled=True)
        both = call(softmax_body, shaped((16, 48, 128), BF), data=2**19, scalars=1)(par, part)
        both = lax.all_to_all(both, ("zh", "zl"), split_axis=0, concat_axis=0, tiled=True)
    with jax.named_scope("mix"):
        i_own, i_send, j_own, j_x, j_core = call(
            mix_body,
            (
                shaped((2,) + units, F32), shaped((2,) + units, BF), shaped((2,) + units, F32),
                shaped((2,) + units, F32), shaped((2, 2) + units, BF),
            ),
            [pltpu.VMEM((16, 48, 128), F32)], flops=4 * 2 * H * 64 * 128 * RE, data=2**22, scalars=1, inputs=8,
        )(par, both, q, qo, da, dao, kv, kvo, kvc)
    with jax.named_scope("exchange_sums"):
        i_recv = lax.ppermute(i_send, X, I_PAIRS)
        j_core = lax.ppermute(j_core, "core", [(0, 1), (1, 0)])
        j_send = call(add_body, shaped((2,) + units, BF), data=2**20, inputs=2)(j_x, j_core)
        j_recv = lax.ppermute(j_send, X, J_PAIRS)
    with jax.named_scope("finish"):
        attended, grad = call(
            finish_body, (shaped((256, HD), BF), shaped((256, D), BF)), [pltpu.VMEM((4, 8, 8, HD), F32)],
            flops=2 * 256 * D * 3 * HD, data=2**22, inputs=8,
        )(i_own, i_recv, j_own, j_core, j_recv, w_query, w_key, w_value)
    with jax.named_scope("to_owners"):
        attended = over_z_hi(attended.reshape(32, 8, HD)).reshape(256, HD)
        layer_out = dot(attended, w_out).astype(BF).reshape(32, 8, D)
        grad = over_z_hi(grad.reshape(32, 8, D))
    return (layer_out, grad)


def solution(mesh):
    fine = Mesh(np.asarray(mesh.devices).reshape(4, 4, 4, 2, 2, 2), ("zl", "y", "zh", "x1", "x0", "core"))
    tokens = P(("zl", "y"), ("zh", "x1", "x0", "core"), None)
    return jax.shard_map(
        shards,
        mesh=fine,
        in_specs=(tokens, tokens, P(), P(), P(), P()),
        out_specs=(tokens, tokens),
        check_vma=False,
    )
```

time: 696 us -> 201 us (0.29)
  the two profiles are of different devices: /device:TPU:1 before, /device:TPU:38 now
where the time goes in v1:
time: 201 us; the launch traced here: 200 us
  blocking collectives  111 us (55%)
  waiting for transfers between devices  50.3 us (25%)
  starting transfers between devices  27.4 us (14%)
  Pallas kernels  4.42 us (2%)
  local copies, waits for them, and re-layouts  2.9 us (1%)
  matrix products  2.18 us (1%)
    all_to_all x2, blocking collectives, over_z_hi(): return lax.all_to_all(a, 'zh', split_axis=0, concat_axis=0, tiled=True)  64 us
    all_to_all x2, waiting for transfers between devices, over_z_hi(): return lax.all_to_all(a, 'zh', split_axis=0, concat_axis=0, tiled=True)  30.1 us
    all_to_all x1, blocking collectives, shards(): lax.all_to_all(both, ('zh', 'zl'), split_axis=0, concat_axis=0, tiled=True)  18.2 us
    all_to_all x1, blocking collectives, shards(): lax.all_to_all(part, ('zh', 'zl'), split_axis=0, concat_axis=0, tiled=True)  17.1 us
    all_to_all x1, blocking collectives, shards(): lax.all_to_all(part, ('y', 'x0'), split_axis=0, concat_axis=0, tiled=True)  11.5 us
    all_to_all x2, starting transfers between devices, over_z_hi(): return lax.all_to_all(a, 'zh', split_axis=0, concat_axis=0, tiled=True)  6.83 us
    ppermute x1, waiting for transfers between devices, shards(): kvo = lax.ppermute(kv, X, J_PAIRS)  6.21 us
    ppermute x1, starting transfers between devices, shards(): j_recv = lax.ppermute(j_send, X, J_PAIRS)  5.44 us
  transfers between devices with their start and end apart: 9, of which 7 were waited for; matrix products, arithmetic and copies ran while one was open for 2% of the time, Pallas kernels for 0%

profile of v1, /device:TPU:38, one launch (start us, length us, event | category | flops | bytes accessed | tf_op | source)
XLA Modules:
  0.0 199.8 jit_solution(15550091553228773135)
XLA Ops:
  0.7 41.3 %all_to_all.35 = bf16[32,8,768]{2,1,0:T(8,128)(2,1)S(1)} all-to-all(bf16[32,8,768]{2,1,0:T(8,128)(2,1)} %param.6), channel_id=1, replica_groups=mesh['zl'=4,'y'=4,'zh'=4,'x1'=2,'x0'=2,'core'=2] {'zh'}, dimensions={0} | all-to-all | bytes 786432 | tf_op jit(solution)/shard_map/layer_in_to_home/all_to_all | solution.py:208
  44.9 2.4 %collective-permute-start.2 = (bf16[2,6,32,512]{3,2,1,0:T(8,128)(2,1)S(1)}, bf16[2,6,32,512]{3,2,1,0:T(8,128)(2,1)S(1)}, u32[]{:S(2)}, u32[]{:S(2)}) collective-permute-start(bf16[2,6,32,512]{3,2,1,0:T(8,128)(2,1)S(1)} %get-tuple-element.12.kv), channel_id=1, source_target_pairs={{0,6},{6,0},{2,4},{4,2},{1,7},{7,1},{3,5},{5,3},{8,14},{14,8},{10,... | collective-permute-start | bytes 1179656 | tf_op jit(solution)/shard_map/exchange_blocks/ppermute | solution.py:222
  47.4 1.1 fusion.1
  48.4 3.4 %all-to-all-start.1 = ((bf16[32,8,384]{2,1,0:T(8,128)(2,1)}), bf16[32,8,384]{2,1,0:T(8,128)(2,1)S(1)}, u32[]{:S(2)}, u32[]{:S(2)}) async-start(bf16[32,8,384]{2,1,0:T(8,128)(2,1)} %fusion.1), calls=%async_computation.1 | async-start | bytes 393216 | tf_op jit(solution)/shard_map/d_att/all_to_all | solution.py:208
  51.8 6.2 %collective-permute-done.2.kvo = bf16[2,6,32,512]{3,2,1,0:T(8,128)(2,1)S(1)} collective-permute-done((bf16[2,6,32,512]{3,2,1,0:T(8,128)(2,1)S(1)}, bf16[2,6,32,512]{3,2,1,0:T(8,128)(2,1)S(1)}, u32[]{:S(2)}, u32[]{:S(2)}) %collective-permute-start.2) | collective-permute-done | bytes 393248 | tf_op jit(solution)/shard_map/exchange_blocks/ppermute | solution.py:222
  59.0 1.9 collective-permute-start.3
  60.9 7.2 %all-to-all-done.1 = bf16[32,8,384]{2,1,0:T(8,128)(2,1)S(1)} async-done(((bf16[32,8,384]{2,1,0:T(8,128)(2,1)}), bf16[32,8,384]{2,1,0:T(8,128)(2,1)S(1)}, u32[]{:S(2)}, u32[]{:S(2)}) %all-to-all-start.1) | async-done | bytes 196640 | tf_op jit(solution)/shard_map/d_att/all_to_all | solution.py:208
  68.2 2.8 %collective-permute-start.1 = (bf16[6,32,512]{2,1,0:T(8,128)(2,1)S(1)}, bf16[6,32,512]{2,1,0:T(8,128)(2,1)S(1)}, u32[]{:S(2)}, u32[]{:S(2)}) collective-permute-start(bf16[6,32,512]{2,1,0:T(8,128)(2,1)S(1)} %project.3.da), channel_id=1, source_target_pairs={{0,2},{2,0},{4,6},{6,4},{1,3},{3,1},{5,7},{7,5},{8,10},{10,8},{12,... | collective-permute-start | bytes 589832 | tf_op jit(solution)/shard_map/exchange_blocks/ppermute | solution.py:223
  71.0 3.0 %collective-permute-start = (bf16[6,32,512]{2,1,0:T(8,128)(2,1)S(1)}, bf16[6,32,512]{2,1,0:T(8,128)(2,1)S(1)}, u32[]{:S(2)}, u32[]{:S(2)}) collective-permute-start(bf16[6,32,512]{2,1,0:T(8,128)(2,1)S(1)} %get-tuple-element.11.q), channel_id=1, source_target_pairs={{0,2},{2,0},{4,6},{6,4},{1,3},{3,1},{5,7},{7,5},{8,10},{10,8},{12,... | collective-permute-start | bytes 589832 | tf_op jit(solution)/shard_map/exchange_blocks/ppermute | solution.py:221
  74.0 1.7 collective-permute-done.1.dao
  75.7 2.8 %collective-permute-done.qo = bf16[6,32,512]{2,1,0:T(8,128)(2,1)S(1)} collective-permute-done((bf16[6,32,512]{2,1,0:T(8,128)(2,1)S(1)}, bf16[6,32,512]{2,1,0:T(8,128)(2,1)S(1)}, u32[]{:S(2)}, u32[]{:S(2)}) %collective-permute-start) | collective-permute-done | bytes 196640 | tf_op jit(solution)/shard_map/exchange_blocks/ppermute | solution.py:221
  79.2 17.1 %all_to_all.36.a_ref = bf16[16,48,128]{2,1,0:T(8,128)(2,1)S(1)} all-to-all(bf16[16,48,128]{2,1,0:T(8,128)(2,1)S(1)} %partial_sums.1), channel_id=1, replica_groups=mesh['zl'=4,'y'=4,'zh'=4,'x1'=2,'x0'=2,'core'=2] {'zh','zl'}, dimensions={0} | all-to-all | bytes 393216 | tf_op jit(solution)/shard_map/reduce/all_to_all | solution.py:231
  96.3 11.5 %all_to_all.37.g_ref = f32[8,48,128]{2,1,0:T(8,128)S(1)} all-to-all(f32[8,48,128]{2,1,0:T(8,128)S(1)} %reduce.2), channel_id=1, replica_groups=mesh['zl'=4,'y'=4,'zh'=4,'x1'=2,'x0'=2,'core'=2] {'y','x0'}, dimensions={0} | all-to-all | bytes 393216 | tf_op jit(solution)/shard_map/reduce/all_to_all | solution.py:233
  108.1 18.2 %all_to_all.38.pd_ref = bf16[16,48,128]{2,1,0:T(8,128)(2,1)S(1)} all-to-all(bf16[16,48,128]{2,1,0:T(8,128)(2,1)S(1)} %reduce.3), channel_id=1, replica_groups=mesh['zl'=4,'y'=4,'zh'=4,'x1'=2,'x0'=2,'core'=2] {'zh','zl'}, dimensions={0} | all-to-all | bytes 393216 | tf_op jit(solution)/shard_map/reduce/all_to_all | solution.py:235
  127.1 1.9 collective-permute-start.5
  129.1 3.1 %collective-permute-start.4 = (bf16[2,6,32,512]{3,2,1,0:T(8,128)(2,1)S(1)}, bf16[2,6,32,512]{3,2,1,0:T(8,128)(2,1)S(1)}, u32[]{:S(2)}, u32[]{:S(2)}) collective-permute-start(bf16[2,6,32,512]{3,2,1,0:T(8,128)(2,1)S(1)} %get-tuple-element.14), channel_id=1, source_target_pairs={{0,2},{2,0},{4,6},{6,4},{1,3},{3,1},{5,7},{7,5},{8,10},{10,8},{12,... | collective-permute-start | bytes 1179656 | tf_op jit(solution)/shard_map/exchange_sums/ppermute | solution.py:246
  132.3 5.4 %collective-permute-start.6 = (bf16[2,6,32,512]{3,2,1,0:T(8,128)(2,1)S(1)}, bf16[2,6,32,512]{3,2,1,0:T(8,128)(2,1)S(1)}, u32[]{:S(2)}, u32[]{:S(2)}) collective-permute-start(bf16[2,6,32,512]{3,2,1,0:T(8,128)(2,1)S(1)} %exchange_sums.1), channel_id=1, source_target_pairs={{0,6},{6,0},{2,4},{4,2},{1,7},{7,1},{3,5},{5,3},{8,14},{14,8},{10,... | collective-permute-start | bytes 1179656 | tf_op jit(solution)/shard_map/exchange_sums/ppermute | solution.py:249
  137.7 4.7 %collective-permute-done.4.i_recv = bf16[2,6,32,512]{3,2,1,0:T(8,128)(2,1)S(1)} collective-permute-done((bf16[2,6,32,512]{3,2,1,0:T(8,128)(2,1)S(1)}, bf16[2,6,32,512]{3,2,1,0:T(8,128)(2,1)S(1)}, u32[]{:S(2)}, u32[]{:S(2)}) %collective-permute-start.4) | collective-permute-done | bytes 393248 | tf_op jit(solution)/shard_map/exchange_sums/ppermute | solution.py:246
  142.5 4.7 %collective-permute-done.6.j_recv = bf16[2,6,32,512]{3,2,1,0:T(8,128)(2,1)S(1)} collective-permute-done((bf16[2,6,32,512]{3,2,1,0:T(8,128)(2,1)S(1)}, bf16[2,6,32,512]{3,2,1,0:T(8,128)(2,1)S(1)}, u32[]{:S(2)}, u32[]{:S(2)}) %collective-permute-start.6) | collective-permute-done | bytes 393248 | tf_op jit(solution)/shard_map/exchange_sums/ppermute | solution.py:249
  147.2 1.6 finish.1
  148.8 22.7 %all_to_all.39 = bf16[32,8,384]{2,1,0:T(8,128)(2,1)S(1)} all-to-all(bf16[32,8,384]{2,1,0:T(8,128)(2,1)S(1)} %bitcast.23), channel_id=1, replica_groups=mesh['zl'=4,'y'=4,'zh'=4,'x1'=2,'x0'=2,'core'=2] {'zh'}, dimensions={0} | all-to-all | bytes 393216 | tf_op jit(solution)/shard_map/to_owners/all_to_all | solution.py:208
  171.5 3.5 %all-to-all-start.6 = ((bf16[32,8,768]{2,1,0:T(8,128)(2,1)}), bf16[32,8,768]{2,1,0:T(8,128)(2,1)S(1)}, u32[]{:S(2)}, u32[]{:S(2)}) async-start(bf16[32,8,768]{2,1,0:T(8,128)(2,1)} %bitcast.10), calls=%async_computation.6 | async-start | bytes 786432 | tf_op jit(solution)/shard_map/to_owners/all_to_all | solution.py:208
  175.0 1.1 fusion
  176.1 22.9 %all-to-all-done.6 = bf16[32,8,768]{2,1,0:T(8,128)(2,1)S(1)} async-done(((bf16[32,8,768]{2,1,0:T(8,128)(2,1)}), bf16[32,8,768]{2,1,0:T(8,128)(2,1)S(1)}, u32[]{:S(2)}, u32[]{:S(2)}) %all-to-all-start.6) | async-done | bytes 393248 | tf_op jit(solution)/shard_map/to_owners/all_to_all | solution.py:208
  (25 shorter events, 6.7 us)
Async XLA Ops:
  0.6 46.7 %copy-start = (bf16[384,768]{1,0:T(8,128)(2,1)S(1)}, bf16[384,768]{1,0:T(8,128)(2,1)}, u32[]{:S(2)}) copy-start(bf16[384,768]{1,0:T(8,128)(2,1)} %param.11) | copy-start | bytes 1769476
  0.6 41.3 %copy-start.1 = (bf16[768,384]{1,0:T(8,128)(2,1)S(1)}, bf16[768,384]{1,0:T(8,128)(2,1)}, u32[]{:S(2)}) copy-start(bf16[768,384]{1,0:T(8,128)(2,1)} %wq_ref.3) | copy-start | bytes 1769476
  42.0 1.1 copy-start.2
  43.0 1.1 copy-start.4
  44.1 3.3 %copy-start.6 = (bf16[32,8,768]{2,1,0:T(8,128)(2,1)S(1)}, bf16[32,8,768]{2,1,0:T(8,128)(2,1)}, u32[]{:S(2)}) copy-start(bf16[32,8,768]{2,1,0:T(8,128)(2,1)} %param.7) | copy-start | bytes 1179652
  44.9 13.1 %collective-permute-start.2 = (bf16[2,6,32,512]{3,2,1,0:T(8,128)(2,1)S(1)}, bf16[2,6,32,512]{3,2,1,0:T(8,128)(2,1)S(1)}, u32[]{:S(2)}, u32[]{:S(2)}) collective-permute-start(bf16[2,6,32,512]{3,2,1,0:T(8,128)(2,1)S(1)} %get-tuple-element.12.kv), channel_id=1, source_target_pairs={{0,6},{6,0},{2,4},{4,2},{1,7},{7,1},{3,5},{5,3},{8,14},{14,8},{10,... | collective-permute-start | bytes 1179656 | tf_op jit(solution)/shard_map/exchange_blocks/ppermute | solution.py:222
  48.4 19.6 %all-to-all-start.1 = ((bf16[32,8,384]{2,1,0:T(8,128)(2,1)}), bf16[32,8,384]{2,1,0:T(8,128)(2,1)S(1)}, u32[]{:S(2)}, u32[]{:S(2)}) async-start(bf16[32,8,384]{2,1,0:T(8,128)(2,1)} %fusion.1), calls=%async_computation.1 | async-start | bytes 393216 | tf_op jit(solution)/shard_map/d_att/all_to_all | solution.py:208
  59.0 19.6 %collective-permute-start.3 = (bf16[2,2,6,32,512]{4,3,2,1,0:T(8,128)(2,1)}, bf16[2,2,6,32,512]{4,3,2,1,0:T(8,128)(2,1)S(1)}, u32[]{:S(2)}, u32[]{:S(2)}) collective-permute-start(bf16[2,2,6,32,512]{4,3,2,1,0:T(8,128)(2,1)} %pad_maximum_fusion), channel_id=1, source_target_pairs={{0,1},{1,0},{2,3},{3,2},{4,5},{5,4},{6,7},{7,6},{8,9},{9,8},{10,11... | collective-permute-start | bytes 2359304 | tf_op jit(solution)/shard_map/exchange_blocks/ppermute | solution.py:224
  68.2 7.6 %collective-permute-start.1 = (bf16[6,32,512]{2,1,0:T(8,128)(2,1)S(1)}, bf16[6,32,512]{2,1,0:T(8,128)(2,1)S(1)}, u32[]{:S(2)}, u32[]{:S(2)}) collective-permute-start(bf16[6,32,512]{2,1,0:T(8,128)(2,1)S(1)} %project.3.da), channel_id=1, source_target_pairs={{0,2},{2,0},{4,6},{6,4},{1,3},{3,1},{5,7},{7,5},{8,10},{10,8},{12,... | collective-permute-start | bytes 589832 | tf_op jit(solution)/shard_map/exchange_blocks/ppermute | solution.py:223
  71.0 7.6 %collective-permute-start = (bf16[6,32,512]{2,1,0:T(8,128)(2,1)S(1)}, bf16[6,32,512]{2,1,0:T(8,128)(2,1)S(1)}, u32[]{:S(2)}, u32[]{:S(2)}) collective-permute-start(bf16[6,32,512]{2,1,0:T(8,128)(2,1)S(1)} %get-tuple-element.11.q), channel_id=1, source_target_pairs={{0,2},{2,0},{4,6},{6,4},{1,3},{3,1},{5,7},{7,5},{8,10},{10,8},{12,... | collective-permute-start | bytes 589832 | tf_op jit(solution)/shard_map/exchange_blocks/ppermute | solution.py:221
  127.1 5.0 %collective-permute-start.5 = (bf16[2,2,6,32,512]{4,3,2,1,0:T(8,128)(2,1)S(1)}, bf16[2,2,6,32,512]{4,3,2,1,0:T(8,128)(2,1)S(1)}, u32[]{:S(2)}, u32[]{:S(2)}) collective-permute-start(bf16[2,2,6,32,512]{4,3,2,1,0:T(8,128)(2,1)S(1)} %get-tuple-element.16), channel_id=1, source_target_pairs={{0,1},{1,0},{2,3},{3,2},{4,5},{5,4},{6,7},{7,6},{8,9},{9,8},{10,11... | collective-permute-start | bytes 2359304 | tf_op jit(solution)/shard_map/exchange_sums/ppermute | solution.py:247
  129.1 13.4 %collective-permute-start.4 = (bf16[2,6,32,512]{3,2,1,0:T(8,128)(2,1)S(1)}, bf16[2,6,32,512]{3,2,1,0:T(8,128)(2,1)S(1)}, u32[]{:S(2)}, u32[]{:S(2)}) collective-permute-start(bf16[2,6,32,512]{3,2,1,0:T(8,128)(2,1)S(1)} %get-tuple-element.14), channel_id=1, source_target_pairs={{0,2},{2,0},{4,6},{6,4},{1,3},{3,1},{5,7},{7,5},{8,10},{10,8},{12,... | collective-permute-start | bytes 1179656 | tf_op jit(solution)/shard_map/exchange_sums/ppermute | solution.py:246
  132.2 15.0 %copy-start.3 = (bf16[768,384]{1,0:T(8,128)(2,1)S(1)}, bf16[768,384]{1,0:T(8,128)(2,1)}, u32[]{:S(2)}) copy-start(bf16[768,384]{1,0:T(8,128)(2,1)} %wk_ref.3) | copy-start | bytes 1769476
  132.2 15.0 %copy-start.5 = (bf16[768,384]{1,0:T(8,128)(2,1)S(1)}, bf16[768,384]{1,0:T(8,128)(2,1)}, u32[]{:S(2)}) copy-start(bf16[768,384]{1,0:T(8,128)(2,1)} %wv_ref.3) | copy-start | bytes 1769476
  132.3 14.9 %collective-permute-start.6 = (bf16[2,6,32,512]{3,2,1,0:T(8,128)(2,1)S(1)}, bf16[2,6,32,512]{3,2,1,0:T(8,128)(2,1)S(1)}, u32[]{:S(2)}, u32[]{:S(2)}) collective-permute-start(bf16[2,6,32,512]{3,2,1,0:T(8,128)(2,1)S(1)} %exchange_sums.1), channel_id=1, source_target_pairs={{0,6},{6,0},{2,4},{4,2},{1,7},{7,1},{3,5},{5,3},{8,14},{14,8},{10,... | collective-permute-start | bytes 1179656 | tf_op jit(solution)/shard_map/exchange_sums/ppermute | solution.py:249
  171.5 27.5 %all-to-all-start.6 = ((bf16[32,8,768]{2,1,0:T(8,128)(2,1)}), bf16[32,8,768]{2,1,0:T(8,128)(2,1)S(1)}, u32[]{:S(2)}, u32[]{:S(2)}) async-start(bf16[32,8,768]{2,1,0:T(8,128)(2,1)} %bitcast.10), calls=%async_computation.6 | async-start | bytes 786432 | tf_op jit(solution)/shard_map/to_owners/all_to_all | solution.py:208

commit v2 on v1

--- a/solution.py
+++ b/solution.py
@@ -15,7 +15,7 @@
 NT = 32
 RE = 512
 SCALING = 1.0 / math.sqrt(DH * 512)
-X = ("x1", "x0")
+Z = ("z1", "z0")
 I_PAIRS = [(0, 1), (1, 0), (2, 3), (3, 2)]
 J_PAIRS = [(0, 3), (3, 0), (1, 2), (2, 1)]
 BF = jnp.bfloat16
@@ -83,8 +83,8 @@
     return jax.ShapeDtypeStruct(shape, dtype)
 
 
-def project_body(x_ref, wq_ref, wk_ref, wv_ref, q_ref, kv_ref):
-    x = x_ref[...]
+def project_body(home_ref, wq_ref, wk_ref, wv_ref, q_ref, kv_ref, da_ref):
+    x = home_ref[:, 0:D]
 
     def put_q(h, pair, block):
         q_ref[h, :, pair * 128 : pair * 128 + 128] = block.astype(BF)
@@ -99,12 +99,10 @@
     tokens_to_heads(dot(x, wk_ref[...]), put_kv(0))
     tokens_to_heads(dot(x, wv_ref[...]), put_kv(1))
 
-
-def relayout_body(a_ref, out_ref):
-    def put(h, pair, block):
-        out_ref[h, :, pair * 128 : pair * 128 + 128] = block.astype(BF)
-
-    tokens_to_heads(a_ref[...].astype(F32), put)
+    def put_da(h, pair, block):
+        da_ref[h, :, pair * 128 : pair * 128 + 128] = block.astype(BF)
+
+    tokens_to_heads(home_ref[:, D:].astype(F32), put_da)
 
 
 def partial_body(par_ref, q, qo, da, dao, kv, kvo, kvc, out_ref, scr):
@@ -117,9 +115,9 @@
             rows = slice((which * 3 + h % 3) * 8, (which * 3 + h % 3) * 8 + 8)
             for side in range(2):
                 place = lax.bitwise_xor(par, side) * 8 + h // 3
-                for zs in range(4):
-                    start = side * NT + zs * 8
-                    scr[place + 2 * zs, rows, :] = part[start : start + 8]
+                for xs in range(4):
+                    start = side * NT + xs * 8
+                    scr[place + 2 * xs, rows, :] = part[start : start + 8]
     out_ref[...] = scr[...].astype(BF)
 
 
@@ -150,16 +148,16 @@
         out_ref[k] = both
 
 
-def mix_body(par_ref, pd_ref, q, qo, da, dao, kv, kvo, kvc, i_own, i_send, j_own, j_x, j_core, scr):
+def mix_body(par_ref, pd_ref, q, qo, da, dao, kv, kvo, kvc, i_own, i_send, j_own, j_z, j_core, scr):
     par = par_ref[0]
     scr[...] = pd_ref[...].astype(F32)
     for h in range(H):
         probs, d_logits = [], []
         for side in range(2):
             place = lax.bitwise_xor(par, side) * 8 + h // 3
-            for zs in range(4):
-                probs.append(scr[place + 2 * zs, (h % 3) * 8 : (h % 3) * 8 + 8, :])
-                d_logits.append(scr[place + 2 * zs, 24 + (h % 3) * 8 : 24 + (h % 3) * 8 + 8, :])
+            for xs in range(4):
+                probs.append(scr[place + 2 * xs, (h % 3) * 8 : (h % 3) * 8 + 8, :])
+                d_logits.append(scr[place + 2 * xs, 24 + (h % 3) * 8 : 24 + (h % 3) * 8 + 8, :])
         prob = jnp.concatenate(probs, axis=0)
         d_logit = jnp.concatenate(d_logits, axis=0)
         keys = jnp.concatenate([kv[0, h], kvo[0, h], kvc[0, 0, h], kvc[1, 0, h]], axis=0)
@@ -175,21 +173,21 @@
             i_send[which, h] = value[NT:].astype(BF)
         for which, value in ((0, d_key), (1, d_value)):
             j_own[which, h] = value[0:NT]
-            j_x[which, h] = value[NT : 2 * NT]
+            j_z[which, h] = value[NT : 2 * NT]
             j_core[0, which, h] = value[2 * NT : 3 * NT].astype(BF)
             j_core[1, which, h] = value[3 * NT :].astype(BF)
 
 
-def add_body(j_x, j_core, out_ref):
-    out_ref[...] = (j_x[...] + j_core[1].astype(F32)).astype(BF)
-
-
-def finish_body(i_own, i_recv, j_own, j_core, j_recv, wq_ref, wk_ref, wv_ref, att_ref, grad_ref, scr):
+def add_body(j_z, j_core, out_ref):
+    out_ref[...] = (j_z[...] + j_core[1].astype(F32)).astype(BF)
+
+
+def finish_body(i_own, i_recv, j_own, j_core, j_recv, wq_ref, wk_ref, wv_ref, out_ref, scr):
     def gather(heads):
         heads_to_tokens(heads, scr)
         return scr[...].reshape(4 * 8 * 8, HD).astype(BF)
 
-    att_ref[...] = gather(lambda h: i_own[0, h] + i_recv[0, h].astype(F32))
+    out_ref[:, D:] = gather(lambda h: i_own[0, h] + i_recv[0, h].astype(F32))
     d_query = gather(lambda h: i_own[1, h] + i_recv[1, h].astype(F32))
     total = dot_t(d_query, wq_ref[...])
     for which, weight in ((0, wk_ref), (1, wv_ref)):
@@ -197,30 +195,28 @@
             lambda h: j_own[which, h] + j_core[0, which, h].astype(F32) + j_recv[which, h].astype(F32)
         )
         total = total + dot_t(grad, weight[...])
-    grad_ref[...] = total.astype(BF)
+    out_ref[:, 0:D] = total.astype(BF)
 
 
 def shards(layer_in, cotangent, w_query, w_key, w_value, w_out):
-    par = lax.axis_index("x0").astype(jnp.int32).reshape(1)
+    par = lax.axis_index("z0").astype(jnp.int32).reshape(1)
     units = (H, NT, RE)
 
-    def over_z_hi(a):
-        return lax.all_to_all(a, "zh", split_axis=0, concat_axis=0, tiled=True)
-
-    with jax.named_scope("layer_in_to_home"):
-        x_home = over_z_hi(layer_in).reshape(256, D)
-    with jax.named_scope("d_att"):
+    def over_x(a):
+        return lax.all_to_all(a, "x", split_axis=0, concat_axis=0, tiled=True)
+
+    with jax.named_scope("to_homes"):
         d_att = dot_t(cotangent.reshape(256, D), w_out).astype(BF).reshape(32, 8, HD)
-        d_att = over_z_hi(d_att).reshape(256, HD)
+        home = over_x(jnp.concatenate([layer_in, d_att], axis=2)).reshape(256, D + HD)
     with jax.named_scope("project"):
-        q, kv = call(
-            project_body, (shaped(units, BF), shaped((2,) + units, BF)), flops=2 * 256 * D * 3 * HD, data=3 * 2**20, inputs=4
-        )(x_home, w_query, w_key, w_value)
-        da = call(relayout_body, shaped(units, BF), data=2**19)(d_att)
+        q, kv, da = call(
+            project_body, (shaped(units, BF), shaped((2,) + units, BF), shaped(units, BF)),
+            flops=2 * 256 * D * 3 * HD, data=3 * 2**20, inputs=4,
+        )(home, w_query, w_key, w_value)
     with jax.named_scope("exchange_blocks"):
-        qo = lax.ppermute(q, X, I_PAIRS)
-        kvo = lax.ppermute(kv, X, J_PAIRS)
-        dao = lax.ppermute(da, X, I_PAIRS)
+        qo = lax.ppermute(q, Z, I_PAIRS)
+        kvo = lax.ppermute(kv, Z, J_PAIRS)
+        dao = lax.ppermute(da, Z, I_PAIRS)
         kvc = lax.ppermute(jnp.stack([kv, kvo]), "core", [(0, 1), (1, 0)])
     with jax.named_scope("partial_sums"):
         part = call(
@@ -228,13 +224,13 @@
             flops=2 * 2 * H * 64 * 128 * RE, data=2**21, scalars=1, inputs=7,
         )(par, q, qo, da, dao, kv, kvo, kvc)
     with jax.named_scope("reduce"):
-        part = lax.all_to_all(part, ("zh", "zl"), split_axis=0, concat_axis=0, tiled=True)
+        part = lax.all_to_all(part, ("y", "x"), split_axis=0, concat_axis=0, tiled=True)
         part = call(sum_body, shaped((8, 48, 128), F32), data=2**19)(part)
-        part = lax.all_to_all(part, ("y", "x0"), split_axis=0, concat_axis=0, tiled=True)
+        part = lax.all_to_all(part, ("zl", "z0"), split_axis=0, concat_axis=0, tiled=True)
         both = call(softmax_body, shaped((16, 48, 128), BF), data=2**19, scalars=1)(par, part)
-        both = lax.all_to_all(both, ("zh", "zl"), split_axis=0, concat_axis=0, tiled=True)
+        both = lax.all_to_all(both, ("y", "x"), split_axis=0, concat_axis=0, tiled=True)
     with jax.named_scope("mix"):
-        i_own, i_send, j_own, j_x, j_core = call(
+        i_own, i_send, j_own, j_z, j_core = call(
             mix_body,
             (
                 shaped((2,) + units, F32), shaped((2,) + units, BF), shaped((2,) + units, F32),
@@ -243,25 +239,25 @@
             [pltpu.VMEM((16, 48, 128), F32)], flops=4 * 2 * H * 64 * 128 * RE, data=2**22, scalars=1, inputs=8,
         )(par, both, q, qo, da, dao, kv, kvo, kvc)
     with jax.named_scope("exchange_sums"):
-        i_recv = lax.ppermute(i_send, X, I_PAIRS)
+        i_recv = lax.ppermute(i_send, Z, I_PAIRS)
         j_core = lax.ppermute(j_core, "core", [(0, 1), (1, 0)])
-        j_send = call(add_body, shaped((2,) + units, BF), data=2**20, inputs=2)(j_x, j_core)
-        j_recv = lax.ppermute(j_send, X, J_PAIRS)
+        j_send = call(add_body, shaped((2,) + units, BF), data=2**20, inputs=2)(j_z, j_core)
+        j_recv = lax.ppermute(j_send, Z, J_PAIRS)
     with jax.named_scope("finish"):
-        attended, grad = call(
-            finish_body, (shaped((256, HD), BF), shaped((256, D), BF)), [pltpu.VMEM((4, 8, 8, HD), F32)],
+        home = call(
+            finish_body, shaped((256, D + HD), BF), [pltpu.VMEM((4, 8, 8, HD), F32)],
             flops=2 * 256 * D * 3 * HD, data=2**22, inputs=8,
         )(i_own, i_recv, j_own, j_core, j_recv, w_query, w_key, w_value)
     with jax.named_scope("to_owners"):
-        attended = over_z_hi(attended.reshape(32, 8, HD)).reshape(256, HD)
-        layer_out = dot(attended, w_out).astype(BF).reshape(32, 8, D)
-        grad = over_z_hi(grad.reshape(32, 8, D))
+        home = over_x(home.reshape(32, 8, D + HD))
+        layer_out = dot(home[:, :, D:].reshape(256, HD), w_out).astype(BF).reshape(32, 8, D)
+        grad = home[:, :, 0:D]
     return (layer_out, grad)
 
 
 def solution(mesh):
-    fine = Mesh(np.asarray(mesh.devices).reshape(4, 4, 4, 2, 2, 2), ("zl", "y", "zh", "x1", "x0", "core"))
-    tokens = P(("zl", "y"), ("zh", "x1", "x0", "core"), None)
+    fine = Mesh(np.asarray(mesh.devices).reshape(4, 4, 2, 2, 4, 2), ("zl", "y", "z1", "z0", "x", "core"))
+    tokens = P(("zl", "y"), ("z1", "z0", "x", "core"), None)
     return jax.shard_map(
         shards,
         mesh=fine,

time: 201 us -> 214 us (1.065)
  the two profiles are of different devices: /device:TPU:38 before, /device:TPU:1 now
where the time goes in v2:
time: 214 us; the launch traced here: 213 us
  waiting for transfers between devices  92.4 us (43%)
  blocking collectives  62.5 us (29%)
  starting transfers between devices  45.8 us (21%)
  Pallas kernels  6.5 us (3%)
  matrix products  2.49 us (1%)
    ppermute x1, waiting for transfers between devices, shards(): kvo = lax.ppermute(kv, Z, J_PAIRS)  33.6 us
    ppermute x1, waiting for transfers between devices, shards(): i_recv = lax.ppermute(i_send, Z, I_PAIRS)  30.1 us
    all_to_all x2, blocking collectives, over_x(): return lax.all_to_all(a, 'x', split_axis=0, concat_axis=0, tiled=True)  23.9 us
    ppermute x1, waiting for transfers between devices, shards(): qo = lax.ppermute(q, Z, I_PAIRS)  20.9 us
    all_to_all x1, blocking collectives, shards(): lax.all_to_all(part, ('zl', 'z0'), split_axis=0, concat_axis=0, tiled=True)  16.5 us
    ppermute x1, starting transfers between devices, shards(): kvo = lax.ppermute(kv, Z, J_PAIRS)  14.1 us
    all_to_all x1, blocking collectives, shards(): lax.all_to_all(part, ('y', 'x'), split_axis=0, concat_axis=0, tiled=True)  11.9 us
    all_to_all x1, blocking collectives, shards(): lax.all_to_all(both, ('y', 'x'), split_axis=0, concat_axis=0, tiled=True)  10.2 us
  transfers between devices with their start and end apart: 7, of which 5 were waited for; matrix products, arithmetic and copies ran while one was open for 0% of the time, Pallas kernels for 0%

profile of v2, /device:TPU:1, one launch (start us, length us, event | category | flops | bytes accessed | tf_op | source)
XLA Modules:
  0.0 213.4 jit_solution(7746119214827063841)
XLA Ops:
  0.7 1.0 copy-done
  1.7 1.4 fusion.1
  3.2 12.1 %all_to_all.25 = bf16[32,8,1152]{2,1,0:T(8,128)(2,1)S(1)} all-to-all(bf16[32,8,1152]{2,1,0:T(8,128)(2,1)S(1)} %pad_maximum_fusion.1), channel_id=1, replica_groups=mesh['zl'=4,'y'=4,'z1'=2,'z0'=2,'x'=4,'core'=2] {'x'}, dimensions={0} | all-to-all | bytes 1179648 | tf_op jit(solution)/shard_map/to_homes/all_to_all | solution.py:206
  15.3 1.5 project.1
  16.8 14.1 %collective-permute-start.2 = (bf16[2,6,32,512]{3,2,1,0:T(8,128)(2,1)S(1)}, bf16[2,6,32,512]{3,2,1,0:T(8,128)(2,1)S(1)}, u32[]{:S(2)}, u32[]{:S(2)}) collective-permute-start(bf16[2,6,32,512]{3,2,1,0:T(8,128)(2,1)S(1)} %get-tuple-element.12.kv), channel_id=1, source_target_pairs={{0,24},{24,0},{8,16},{16,8},{1,25},{25,1},{9,17},{17,9},{2,26},{26... | collective-permute-start | bytes 1179656 | tf_op jit(solution)/shard_map/exchange_blocks/ppermute | solution.py:218
  30.9 33.6 %collective-permute-done.2.kvo = bf16[2,6,32,512]{3,2,1,0:T(8,128)(2,1)S(1)} collective-permute-done((bf16[2,6,32,512]{3,2,1,0:T(8,128)(2,1)S(1)}, bf16[2,6,32,512]{3,2,1,0:T(8,128)(2,1)S(1)}, u32[]{:S(2)}, u32[]{:S(2)}) %collective-permute-start.2) | collective-permute-done | bytes 393248 | tf_op jit(solution)/shard_map/exchange_blocks/ppermute | solution.py:218
  64.5 1.0 pad_maximum_fusion
  65.5 2.9 %collective-permute-start.3 = (bf16[2,2,6,32,512]{4,3,2,1,0:T(8,128)(2,1)}, bf16[2,2,6,32,512]{4,3,2,1,0:T(8,128)(2,1)S(1)}, u32[]{:S(2)}, u32[]{:S(2)}) collective-permute-start(bf16[2,2,6,32,512]{4,3,2,1,0:T(8,128)(2,1)} %pad_maximum_fusion), channel_id=1, source_target_pairs={{0,1},{1,0},{2,3},{3,2},{4,5},{5,4},{6,7},{7,6},{8,9},{9,8},{10,11... | collective-permute-start | bytes 2359304 | tf_op jit(solution)/shard_map/exchange_blocks/ppermute | solution.py:220
  68.4 5.9 %collective-permute-start = (bf16[6,32,512]{2,1,0:T(8,128)(2,1)S(1)}, bf16[6,32,512]{2,1,0:T(8,128)(2,1)}, u32[]{:S(2)}, u32[]{:S(2)}) collective-permute-start(bf16[6,32,512]{2,1,0:T(8,128)(2,1)S(1)} %get-tuple-element.10.q), channel_id=1, source_target_pairs={{0,8},{8,0},{16,24},{24,16},{1,9},{9,1},{17,25},{25,17},{2,10},{10... | collective-permute-start | bytes 589832 | tf_op jit(solution)/shard_map/exchange_blocks/ppermute | solution.py:217
  74.3 3.3 %collective-permute-start.1 = (bf16[6,32,512]{2,1,0:T(8,128)(2,1)}, bf16[6,32,512]{2,1,0:T(8,128)(2,1)}, u32[]{:S(2)}, u32[]{:S(2)}) collective-permute-start(bf16[6,32,512]{2,1,0:T(8,128)(2,1)} %get-tuple-element.11.da), channel_id=1, source_target_pairs={{0,8},{8,0},{16,24},{24,16},{1,9},{9,1},{17,25},{25,17},{2,10},{10... | collective-permute-start | bytes 589832 | tf_op jit(solution)/shard_map/exchange_blocks/ppermute | solution.py:219
  77.6 20.9 %collective-permute-done.qo = bf16[6,32,512]{2,1,0:T(8,128)(2,1)} collective-permute-done((bf16[6,32,512]{2,1,0:T(8,128)(2,1)S(1)}, bf16[6,32,512]{2,1,0:T(8,128)(2,1)}, u32[]{:S(2)}, u32[]{:S(2)}) %collective-permute-start) | collective-permute-done | bytes 196640 | tf_op jit(solution)/shard_map/exchange_blocks/ppermute | solution.py:217
  98.5 4.2 %collective-permute-done.1.dao = bf16[6,32,512]{2,1,0:T(8,128)(2,1)} collective-permute-done((bf16[6,32,512]{2,1,0:T(8,128)(2,1)}, bf16[6,32,512]{2,1,0:T(8,128)(2,1)}, u32[]{:S(2)}, u32[]{:S(2)}) %collective-permute-start.1) | collective-permute-done | bytes 196640 | tf_op jit(solution)/shard_map/exchange_blocks/ppermute | solution.py:219
  102.8 1.8 partial_sums.1
  104.5 11.9 %all_to_all.26.a_ref = bf16[16,48,128]{2,1,0:T(8,128)(2,1)S(1)} all-to-all(bf16[16,48,128]{2,1,0:T(8,128)(2,1)S(1)} %partial_sums.1), channel_id=1, replica_groups=mesh['zl'=4,'y'=4,'z1'=2,'z0'=2,'x'=4,'core'=2] {'y','x'}, dimensions={0} | all-to-all | bytes 393216 | tf_op jit(solution)/shard_map/reduce/all_to_all | solution.py:227
  116.5 16.5 %all_to_all.27.g_ref = f32[8,48,128]{2,1,0:T(8,128)S(1)} all-to-all(f32[8,48,128]{2,1,0:T(8,128)S(1)} %reduce.2), channel_id=1, replica_groups=mesh['zl'=4,'y'=4,'z1'=2,'z0'=2,'x'=4,'core'=2] {'zl','z0'}, dimensions={0} | all-to-all | bytes 393216 | tf_op jit(solution)/shard_map/reduce/all_to_all | solution.py:229
  133.3 10.2 %all_to_all.28.pd_ref = bf16[16,48,128]{2,1,0:T(8,128)(2,1)S(1)} all-to-all(bf16[16,48,128]{2,1,0:T(8,128)(2,1)S(1)} %reduce.3), channel_id=1, replica_groups=mesh['zl'=4,'y'=4,'z1'=2,'z0'=2,'x'=4,'core'=2] {'y','x'}, dimensions={0} | all-to-all | bytes 393216 | tf_op jit(solution)/shard_map/reduce/all_to_all | solution.py:231
  143.5 1.9 mix.1
  145.4 8.3 %collective-permute-start.5 = (bf16[2,2,6,32,512]{4,3,2,1,0:T(8,128)(2,1)S(1)}, bf16[2,2,6,32,512]{4,3,2,1,0:T(8,128)(2,1)S(1)}, u32[]{:S(2)}, u32[]{:S(2)}) collective-permute-start(bf16[2,2,6,32,512]{4,3,2,1,0:T(8,128)(2,1)S(1)} %get-tuple-element.16), channel_id=1, source_target_pairs={{0,1},{1,0},{2,3},{3,2},{4,5},{5,4},{6,7},{7,6},{8,9},{9,8},{10,11... | collective-permute-start | bytes 2359304 | tf_op jit(solution)/shard_map/exchange_sums/ppermute | solution.py:243
  153.7 1.9 collective-permute-start.4
  155.7 9.4 %collective-permute-start.6 = (bf16[2,6,32,512]{3,2,1,0:T(8,128)(2,1)S(1)}, bf16[2,6,32,512]{3,2,1,0:T(8,128)(2,1)S(1)}, u32[]{:S(2)}, u32[]{:S(2)}) collective-permute-start(bf16[2,6,32,512]{3,2,1,0:T(8,128)(2,1)S(1)} %exchange_sums.1), channel_id=1, source_target_pairs={{0,24},{24,0},{8,16},{16,8},{1,25},{25,1},{9,17},{17,9},{2,26},{26... | collective-permute-start | bytes 1179656 | tf_op jit(solution)/shard_map/exchange_sums/ppermute | solution.py:245
  165.1 30.1 %collective-permute-done.4.i_recv = bf16[2,6,32,512]{3,2,1,0:T(8,128)(2,1)S(1)} collective-permute-done((bf16[2,6,32,512]{3,2,1,0:T(8,128)(2,1)S(1)}, bf16[2,6,32,512]{3,2,1,0:T(8,128)(2,1)S(1)}, u32[]{:S(2)}, u32[]{:S(2)}) %collective-permute-start.4) | collective-permute-done | bytes 393248 | tf_op jit(solution)/shard_map/exchange_sums/ppermute | solution.py:242
  195.2 3.6 %collective-permute-done.6.j_recv = bf16[2,6,32,512]{3,2,1,0:T(8,128)(2,1)S(1)} collective-permute-done((bf16[2,6,32,512]{3,2,1,0:T(8,128)(2,1)S(1)}, bf16[2,6,32,512]{3,2,1,0:T(8,128)(2,1)S(1)}, u32[]{:S(2)}, u32[]{:S(2)}) %collective-permute-start.6) | collective-permute-done | bytes 393248 | tf_op jit(solution)/shard_map/exchange_sums/ppermute | solution.py:245
  199.7 11.8 %all_to_all.29 = bf16[32,8,1152]{2,1,0:T(8,128)(2,1)S(1)} all-to-all(bf16[32,8,1152]{2,1,0:T(8,128)(2,1)S(1)} %bitcast.19), channel_id=1, replica_groups=mesh['zl'=4,'y'=4,'z1'=2,'z0'=2,'x'=4,'core'=2] {'x'}, dimensions={0} | all-to-all | bytes 1179648 | tf_op jit(solution)/shard_map/to_owners/all_to_all | solution.py:206
  212.3 1.1 fusion
  (19 shorter events, 2.1 us)
Async XLA Ops:
  0.6 1.1 copy-start
  0.6 2.4 %copy-start.5 = (bf16[32,8,768]{2,1,0:T(8,128)(2,1)S(1)}, bf16[32,8,768]{2,1,0:T(8,128)(2,1)}, u32[]{:S(2)}) copy-start(bf16[32,8,768]{2,1,0:T(8,128)(2,1)} %param.6) | copy-start | bytes 1179652
  3.1 12.2 %copy-start.3 = (bf16[768,384]{1,0:T(8,128)(2,1)S(1)}, bf16[768,384]{1,0:T(8,128)(2,1)}, u32[]{:S(2)}) copy-start(bf16[768,384]{1,0:T(8,128)(2,1)} %wv_ref.3) | copy-start | bytes 1769476
  3.2 12.1 %copy-start.1 = (bf16[768,384]{1,0:T(8,128)(2,1)S(1)}, bf16[768,384]{1,0:T(8,128)(2,1)}, u32[]{:S(2)}) copy-start(bf16[768,384]{1,0:T(8,128)(2,1)} %wq_ref.3) | copy-start | bytes 1769476
  3.2 12.1 %copy-start.2 = (bf16[768,384]{1,0:T(8,128)(2,1)S(1)}, bf16[768,384]{1,0:T(8,128)(2,1)}, u32[]{:S(2)}) copy-start(bf16[768,384]{1,0:T(8,128)(2,1)} %wk_ref.3) | copy-start | bytes 1769476
  16.8 47.7 %collective-permute-start.2 = (bf16[2,6,32,512]{3,2,1,0:T(8,128)(2,1)S(1)}, bf16[2,6,32,512]{3,2,1,0:T(8,128)(2,1)S(1)}, u32[]{:S(2)}, u32[]{:S(2)}) collective-permute-start(bf16[2,6,32,512]{3,2,1,0:T(8,128)(2,1)S(1)} %get-tuple-element.12.kv), channel_id=1, source_target_pairs={{0,24},{24,0},{8,16},{16,8},{1,25},{25,1},{9,17},{17,9},{2,26},{26... | collective-permute-start | bytes 1179656 | tf_op jit(solution)/shard_map/exchange_blocks/ppermute | solution.py:218
  65.5 37.3 %collective-permute-start.3 = (bf16[2,2,6,32,512]{4,3,2,1,0:T(8,128)(2,1)}, bf16[2,2,6,32,512]{4,3,2,1,0:T(8,128)(2,1)S(1)}, u32[]{:S(2)}, u32[]{:S(2)}) collective-permute-start(bf16[2,2,6,32,512]{4,3,2,1,0:T(8,128)(2,1)} %pad_maximum_fusion), channel_id=1, source_target_pairs={{0,1},{1,0},{2,3},{3,2},{4,5},{5,4},{6,7},{7,6},{8,9},{9,8},{10,11... | collective-permute-start | bytes 2359304 | tf_op jit(solution)/shard_map/exchange_blocks/ppermute | solution.py:220
  68.4 30.1 %collective-permute-start = (bf16[6,32,512]{2,1,0:T(8,128)(2,1)S(1)}, bf16[6,32,512]{2,1,0:T(8,128)(2,1)}, u32[]{:S(2)}, u32[]{:S(2)}) collective-permute-start(bf16[6,32,512]{2,1,0:T(8,128)(2,1)S(1)} %get-tuple-element.10.q), channel_id=1, source_target_pairs={{0,8},{8,0},{16,24},{24,16},{1,9},{9,1},{17,25},{25,17},{2,10},{10... | collective-permute-start | bytes 589832 | tf_op jit(solution)/shard_map/exchange_blocks/ppermute | solution.py:217
  74.3 28.4 %collective-permute-start.1 = (bf16[6,32,512]{2,1,0:T(8,128)(2,1)}, bf16[6,32,512]{2,1,0:T(8,128)(2,1)}, u32[]{:S(2)}, u32[]{:S(2)}) collective-permute-start(bf16[6,32,512]{2,1,0:T(8,128)(2,1)} %get-tuple-element.11.da), channel_id=1, source_target_pairs={{0,8},{8,0},{16,24},{24,16},{1,9},{9,1},{17,25},{25,17},{2,10},{10... | collective-permute-start | bytes 589832 | tf_op jit(solution)/shard_map/exchange_blocks/ppermute | solution.py:219
  145.4 10.2 %collective-permute-start.5 = (bf16[2,2,6,32,512]{4,3,2,1,0:T(8,128)(2,1)S(1)}, bf16[2,2,6,32,512]{4,3,2,1,0:T(8,128)(2,1)S(1)}, u32[]{:S(2)}, u32[]{:S(2)}) collective-permute-start(bf16[2,2,6,32,512]{4,3,2,1,0:T(8,128)(2,1)S(1)} %get-tuple-element.16), channel_id=1, source_target_pairs={{0,1},{1,0},{2,3},{3,2},{4,5},{5,4},{6,7},{7,6},{8,9},{9,8},{10,11... | collective-permute-start | bytes 2359304 | tf_op jit(solution)/shard_map/exchange_sums/ppermute | solution.py:243
  153.7 41.5 %collective-permute-start.4 = (bf16[2,6,32,512]{3,2,1,0:T(8,128)(2,1)S(1)}, bf16[2,6,32,512]{3,2,1,0:T(8,128)(2,1)S(1)}, u32[]{:S(2)}, u32[]{:S(2)}) collective-permute-start(bf16[2,6,32,512]{3,2,1,0:T(8,128)(2,1)S(1)} %get-tuple-element.14), channel_id=1, source_target_pairs={{0,8},{8,0},{16,24},{24,16},{1,9},{9,1},{17,25},{25,17},{2,10},{10... | collective-permute-start | bytes 1179656 | tf_op jit(solution)/shard_map/exchange_sums/ppermute | solution.py:242
  155.6 43.2 %copy-start.4 = (bf16[768,384]{1,0:T(8,128)(2,1)S(1)}, bf16[768,384]{1,0:T(8,128)(2,1)}, u32[]{:S(2)}) copy-start(bf16[768,384]{1,0:T(8,128)(2,1)} %wv_ref.3) | copy-start | bytes 1769476
  155.7 43.1 %collective-permute-start.6 = (bf16[2,6,32,512]{3,2,1,0:T(8,128)(2,1)S(1)}, bf16[2,6,32,512]{3,2,1,0:T(8,128)(2,1)S(1)}, u32[]{:S(2)}, u32[]{:S(2)}) collective-permute-start(bf16[2,6,32,512]{3,2,1,0:T(8,128)(2,1)S(1)} %exchange_sums.1), channel_id=1, source_target_pairs={{0,24},{24,0},{8,16},{16,8},{1,25},{25,1},{9,17},{17,9},{2,26},{26... | collective-permute-start | bytes 1179656 | tf_op jit(solution)/shard_map/exchange_sums/ppermute | solution.py:245
